TPU v7x, 256 devices: a whole 4x4x8 slice. The times are simulated.
256 devices in a mesh: dp: 16 (over x_hi, y, core), mp: 16 (over z, x_lo).
Axes of the slice: x: 4 (x_hi: 2, x_lo: 2; x = x_hi * 2 + x_lo), y: 4, z: 8, core: 2. Of those that a mesh axis runs over, the one named last changes fastest.
Arguments:
- tokens: bfloat16 [8192, 6144], P(('dp', 'mp')), may hold values from -40 to 40
- norm_gain: float32 [6144], replicated, may hold values from 0.1 to 1.9
- q_gain: float32 [128], replicated, may hold values from 0.5 to 8
- k_gain: float32 [128], replicated, may hold values from 0.5 to 8
- w_query: bfloat16 [6144, 4096], P('dp', 'mp'), may hold values from -0.078125 to 0.078125
- w_key: bfloat16 [6144, 4096], P('dp', 'mp'), may hold values from -0.078125 to 0.078125
- w_value: bfloat16 [6144, 4096], P('dp', 'mp'), may hold values from -0.078125 to 0.078125
- grad_heads: bfloat16 [8192, 4096], P('dp', 'mp'), may hold values from -6 to 6
Outputs:
- grad_tokens: bfloat16 [8192, 6144], P(('dp', 'mp'))
- grad_query_weight: bfloat16 [6144, 4096], P('dp', 'mp')
- grad_key_weight: bfloat16 [6144, 4096], P('dp', 'mp')
- grad_value_weight: bfloat16 [6144, 4096], P('dp', 'mp')
All inputs are finite; a program needn't handle non-finite values.
Results may differ from a plain program's by a relative error of at most 0.03.
The roundings to bfloat16 on the way count: a program that leaves them out, or rounds other values in their place, can miss the bound.
Values may be sent and summed in bfloat16 or wider, within the bound.
A program may use at most 128 MiB of HBM per device.

v0:
```python
import jax
import jax.numpy as jnp
from jax import lax
from jax.sharding import PartitionSpec as P

PATCH = 256


def normalize(row_data, gain_vector):
    average = jnp.mean(row_data, axis=-1, keepdims=True)
    centred = row_data - average
    inv_spread = lax.rsqrt(jnp.mean(centred * centred, axis=-1, keepdims=True) + 1e-06)
    unit_data = centred * inv_spread
    return (unit_data * gain_vector, unit_data, inv_spread)


def normalize_back(grad_out, unit_data, inv_spread, gain_vector):
    scaled = grad_out * gain_vector
    inner_term = jnp.mean(scaled * unit_data, axis=-1, keepdims=True)
    return (scaled - jnp.mean(scaled, axis=-1, keepdims=True) - unit_data * inner_term) * inv_spread


def attend_first(query_bf, key_bf, grad_out):
    factor = query_bf.shape[-1] ** (-0.5)
    scores = (
        jnp.einsum("bqhd,bkhd->bhqk", query_bf, key_bf, preferred_element_type=jnp.float32) * factor
    )
    attention = jax.nn.softmax(scores, axis=-1)
    attention_bf = attention.astype(jnp.bfloat16)
    grad_value = jnp.einsum(
        "bhqk,bqhd->bkhd", attention_bf, grad_out, preferred_element_type=jnp.float32
    ).astype(jnp.bfloat16)
    return (attention, grad_value)


def attend_rest(attention, query_bf, key_bf, value_bf, grad_out):
    factor = query_bf.shape[-1] ** (-0.5)
    grad_probs = jnp.einsum(
        "bqhd,bkhd->bhqk", grad_out, value_bf, preferred_element_type=jnp.float32
    )
    row_delta = jnp.sum(attention * grad_probs, axis=-1, keepdims=True)
    grad_scores = (attention * (grad_probs - row_delta) * factor).astype(jnp.bfloat16)
    grad_query = jnp.einsum(
        "bhqk,bkhd->bqhd", grad_scores, key_bf, preferred_element_type=jnp.float32
    )
    grad_key = jnp.einsum(
        "bhqk,bqhd->bkhd", grad_scores, query_bf, preferred_element_type=jnp.float32
    )
    return (grad_query, grad_key)


def weight_term(normed_all, grad_list):
    products = [
        lax.dot_general(
            normed_all, grad_item, (((0,), (0,)), ((), ())), preferred_element_type=jnp.float32
        )
        for grad_item in grad_list
    ]
    return jnp.concatenate(products, axis=1)


def per_device(tokens, norm_gain, q_gain, k_gain, w_query, w_key, w_value, grad_heads):
    model_width = tokens.shape[1]
    head_size = q_gain.shape[0]
    local_cols = w_query.shape[1]
    local_heads = local_cols // head_size
    normed_own, unit_rows, row_spread = normalize(tokens.astype(jnp.float32), norm_gain)
    normed_all = lax.all_gather(normed_own.astype(jnp.bfloat16), "mp", axis=0, tiled=True)
    group_tokens = normed_all.shape[0]
    image_count = group_tokens // PATCH
    full_query, full_key, full_value = (
        lax.all_gather(w_query, "dp", axis=0, tiled=True),
        lax.all_gather(w_key, "dp", axis=0, tiled=True),
        lax.all_gather(w_value, "dp", axis=0, tiled=True),
    )
    queries = jnp.dot(normed_all, full_query, preferred_element_type=jnp.float32)
    key_proj = jnp.dot(normed_all, full_key, preferred_element_type=jnp.float32)
    values = jnp.dot(normed_all, full_value, preferred_element_type=jnp.float32).astype(
        jnp.bfloat16
    )
    layout = (image_count, PATCH, local_heads, head_size)
    query_normed, query_unit, query_spread = normalize(queries.reshape(layout), q_gain)
    key_normed, key_unit, key_spread = normalize(key_proj.reshape(layout), k_gain)
    query_bf = query_normed.astype(jnp.bfloat16)
    key_bf = key_normed.astype(jnp.bfloat16)
    grad_out = grad_heads.reshape(layout)
    attention, grad_value = attend_first(query_bf, key_bf, grad_out)
    grad_value = grad_value.reshape(group_tokens, local_cols)
    grad_qn, grad_kn = attend_rest(attention, query_bf, key_bf, values.reshape(layout), grad_out)
    grad_query = (
        normalize_back(grad_qn, query_unit, query_spread, q_gain)
        .astype(jnp.bfloat16)
        .reshape(group_tokens, local_cols)
    )
    grad_key = (
        normalize_back(grad_kn, key_unit, key_spread, k_gain)
        .astype(jnp.bfloat16)
        .reshape(group_tokens, local_cols)
    )
    grad_list = (grad_query, grad_key, grad_value)
    full_weights = (full_query, full_key, full_value)
    running = jnp.zeros((tokens.shape[0] * lax.axis_size("mp"), model_width), jnp.float32)
    for grad_item, weight_item in zip(grad_list, full_weights):
        running = running + lax.dot_general(
            grad_item, weight_item, (((1,), (1,)), ((), ())), preferred_element_type=jnp.float32
        )
    grad_normed = lax.psum_scatter(
        running.astype(jnp.bfloat16), "mp", scatter_dimension=0, tiled=True
    ).astype(jnp.float32)
    grad_tokens = normalize_back(grad_normed, unit_rows, row_spread, norm_gain).astype(jnp.bfloat16)
    stacked = lax.psum_scatter(
        weight_term(normed_all, grad_list).astype(jnp.bfloat16),
        "dp",
        scatter_dimension=0,
        tiled=True,
    ).astype(jnp.float32)
    pieces = (
        stacked[:, :local_cols],
        stacked[:, local_cols : 2 * local_cols],
        stacked[:, 2 * local_cols :],
    )
    return (
        grad_tokens,
        pieces[0].astype(jnp.bfloat16),
        pieces[1].astype(jnp.bfloat16),
        pieces[2].astype(jnp.bfloat16),
    )


def solution(mesh):
    placed = (
        P(("dp", "mp"), None),
        P(),
        P(),
        P(),
        P("dp", "mp"),
        P("dp", "mp"),
        P("dp", "mp"),
        P("dp", "mp"),
    )
    return jax.shard_map(
        per_device,
        mesh=mesh,
        in_specs=placed,
        out_specs=(P(("dp", "mp"), None), P("dp", "mp"), P("dp", "mp"), P("dp", "mp")),
        check_vma=False,
    )
```

profile of v0, /device:TPU:32, one launch (start us, length us, event | category | flops | bytes accessed | tf_op | source)
XLA Modules:
  0.0 638.8 jit_solution(9323153413317472502)
XLA Ops:
  10.4 1.9 fusion.20
  14.7 54.4 %all-gather.9.cloned.1.call-done = bf16[6144,256]{1,0:T(8,128)(2,1)} async-done(((bf16[384,256]{1,0:T(8,128)(2,1)}), bf16[6144,256]{1,0:T(8,128)(2,1)}) %all-gather.9.cloned.1.call-update) | async-done | bytes 3145744 | tf_op jit(solution)/shard_map/all_gather | solution.py:72
  69.2 141.5 %all-gather.5.cloned.1.call-done = bf16[512,6144]{1,0:T(8,128)(2,1)} async-done(((bf16[32,6144]{1,0:T(8,128)(2,1)}), bf16[512,6144]{1,0:T(8,128)(2,1)}) %all-gather.5.cloned.1.call-update) | async-done | bytes 6291472 | tf_op jit(solution)/shard_map/all_gather | solution.py:68
  210.7 5.5 fusion.62
  217.3 53.0 %all-gather.7.cloned.1.call-done = bf16[6144,256]{1,0:T(8,128)(2,1)} async-done(((bf16[384,256]{1,0:T(8,128)(2,1)}), bf16[6144,256]{1,0:T(8,128)(2,1)}) %all-gather.7.cloned.1.call-update) | async-done | bytes 3145744 | tf_op jit(solution)/shard_map/all_gather | solution.py:73
  270.2 5.5 fusion.61
  276.9 50.6 %all-gather.11.cloned.1.call-done = bf16[6144,256]{1,0:T(8,128)(2,1)} async-done(((bf16[384,256]{1,0:T(8,128)(2,1)}), bf16[6144,256]{1,0:T(8,128)(2,1)}) %all-gather.11.cloned.1.call-update) | async-done | bytes 3145744 | tf_op jit(solution)/shard_map/all_gather | solution.py:74
  327.5 5.5 convolution_convert_fusion.3
  334.0 1.5 fusion.56
  335.5 1.5 fusion.10
  337.0 2.0 fusion.53
  339.0 2.1 fusion.54
  343.7 8.4 %fusion.33 = f32[512,6144]{1,0:T(8,128)} fusion(bf16[6144,256]{1,0:T(8,128)(2,1)} %all-gather.7.cloned.1.call-done, bf16[64,8,2,128]{3,2,1,0:T(2,128)(2,1)S(1)} %bitcast.50), kind=kOutput, calls=%fused_computation.57 | convolution fusion | flops 1610612736 | bytes 15990784 | tf_op jit(solution)/shard_map/dot_general | solution.py:104
  352.1 6.5 %fusion.36 = f32[512,6144]{1,0:T(8,128)} fusion(bf16[6144,256]{1,0:T(8,128)(2,1)S(1)} %copy-done.2, bf16[64,8,2,128]{3,2,1,0:T(2,128)(2,1)S(1)} %bitcast.52), kind=kOutput, calls=%fused_computation.60 | convolution fusion | flops 1610612736 | bytes 15990784 | tf_op jit(solution)/shard_map/dot_general | solution.py:104
  358.6 12.1 %add_convert_fusion = bf16[512,6144]{1,0:T(8,128)(2,1)} fusion(f32[512,6144]{1,0:T(8,128)} %fusion.36, f32[512,6144]{1,0:T(8,128)} %fusion.33, bf16[6144,256]{1,0:T(8,128)(2,1)S(1)} %copy-done.1, bf16[64,8,2,128]{3,2,1,0:T(2,128)(2,1)S(1)} %bitcast.48), kind=kOutput, calls=%fused_computation.2 | convolution fusion | flops 1620049920 | bytes 34865152 | tf_op jit(solution)/shard_map/dot_general | solution.py:104
  371.6 4.8 convolution_convert_fusion.2
  376.5 4.8 convolution_convert_fusion.1
  381.3 1.9 convolution_convert_fusion
  383.1 4.2 pad_maximum_fusion
  387.4 12.7 %copy.108 = bf16[6144,768]{1,0:T(8,128)(2,1)} copy(bf16[6144,768]{0,1:T(8,128)(2,1)} %pad_maximum_fusion) | data formatting | bytes 18874368
  400.1 110.0 %reduce-scatter.5.cloned.1.call-done = bf16[32,6144]{1,0:T(8,128)(2,1)} async-done(((bf16[512,6144]{1,0:T(8,128)(2,1)}), bf16[32,6144]{1,0:T(8,128)(2,1)}) %reduce-scatter.5.cloned.1.call-update) | async-done | bytes 393232 | tf_op jit(solution)/shard_map/reduce_scatter | solution.py:107
  511.4 2.0 fusion.24
  513.5 116.6 %reduce-scatter.7.cloned.1.call-done = bf16[384,768]{1,0:T(8,128)(2,1)} async-done(((bf16[6144,768]{1,0:T(8,128)(2,1)}), bf16[384,768]{1,0:T(8,128)(2,1)}) %reduce-scatter.7.cloned.1.call-update) | async-done | bytes 589840
  630.0 1.9 fusion.55
  (71 shorter events, 13.5 us)
Async XLA Ops:
  7.2 62.0 %all-gather.9.cloned.1.call-start = ((), (), s32[]{:S(2)}) async-start(), calls=%async_computation.4 | async-start | bytes 3342336 | tf_op jit(solution)/shard_map/all_gather | solution.py:72
  7.9 202.8 %all-gather.5.cloned.1.call-start = ((), (), s32[]{:S(2)}) async-start(), calls=%async_computation.2 | async-start | bytes 6684672 | tf_op jit(solution)/shard_map/all_gather | solution.py:68
  12.4 257.9 %all-gather.7.cloned.1.call-start = ((), (), s32[]{:S(2)}) async-start(), calls=%async_computation.3 | async-start | bytes 3342336 | tf_op jit(solution)/shard_map/all_gather | solution.py:73
  13.1 314.4 %all-gather.11.cloned.1.call-start = ((), (), s32[]{:S(2)}) async-start(), calls=%async_computation.5 | async-start | bytes 3342336 | tf_op jit(solution)/shard_map/all_gather | solution.py:74
  13.7 496.4 %reduce-scatter.5.cloned.1.call-start = ((), (), s32[]{:S(2)}) async-start(), calls=%async_computation.6 | async-start | bytes 6684672 | tf_op jit(solution)/shard_map/reduce_scatter | solution.py:107
  276.9 57.0 %copy-start.8 = (f32[128]{0:T(128)S(1)}, f32[128]{0:T(128)}, u32[]{:S(2)}) copy-start(f32[128]{0:T(128)} %param.11) | copy-start | bytes 1540
  276.9 57.0 %copy-start.9 = (f32[128]{0:T(128)S(1)}, f32[128]{0:T(128)}, u32[]{:S(2)}) copy-start(f32[128]{0:T(128)} %param.10) | copy-start | bytes 1540
  342.6 9.5 %copy-start.3 = (bf16[2,256,2,128]{3,2,1,0:T(2,128)(2,1)}, bf16[2,256,2,128]{3,2,1,0:T(2,128)(2,1)S(1)}, u32[]{:S(2)}) copy-start(bf16[2,256,2,128]{3,2,1,0:T(2,128)(2,1)S(1)} %copy.98) | copy-start | bytes 786436
  343.7 8.5 %copy-start.2 = (bf16[6144,256]{1,0:T(8,128)(2,1)S(1)}, bf16[6144,256]{1,0:T(8,128)(2,1)}, u32[]{:S(2)}) copy-start(bf16[6144,256]{1,0:T(8,128)(2,1)} %all-gather.9.cloned.1.call-done) | copy-start | bytes 9437188
  343.7 8.5 %copy-start.5 = (bf16[2,256,2,128]{3,2,1,0:T(2,128)(2,1)S(1)}, bf16[2,256,2,128]{3,2,1,0:T(2,128)(2,1)}, u32[]{:S(2)}) copy-start(bf16[2,256,2,128]{3,2,1,0:T(2,128)(2,1)} %copy.96) | copy-start | bytes 786436
  352.1 6.5 %copy-start.1 = (bf16[6144,256]{1,0:T(8,128)(2,1)S(1)}, bf16[6144,256]{1,0:T(8,128)(2,1)}, u32[]{:S(2)}) copy-start(bf16[6144,256]{1,0:T(8,128)(2,1)} %all-gather.11.cloned.1.call-done) | copy-start | bytes 9437188
  370.7 0.9 copy-start.6
  370.7 5.7 copy-start.4
  370.7 259.3 %reduce-scatter.7.cloned.1.call-start = ((), (), s32[]{:S(2)}) async-start(), calls=%async_computation.7 | async-start | bytes 10027008
  371.6 9.6 %slice-start = ((s8[6291456]{0:T(1024)(128)(4,1)}), s8[4194304]{0:T(1024)(128)(4,1)S(1)}, s32[]{:S(2)}) async-start(s8[6291456]{0:T(1024)(128)(4,1)} %bitcast.54), calls=%async_computation.8 | async-start | bytes 8388608
  376.4 4.8 slice-start.1
  400.1 110.0 %copy-start = (bf16[32,6144]{1,0:T(8,128)(2,1)S(1)}, bf16[32,6144]{1,0:T(8,128)(2,1)}, u32[]{:S(2)}) copy-start(bf16[32,6144]{1,0:T(8,128)(2,1)} %param.8) | copy-start | bytes 1179652
  400.1 110.0 %copy-start.7 = (f32[6144]{0:T(1024)S(1)}, f32[6144]{0:T(1024)}, u32[]{:S(2)}) copy-start(f32[6144]{0:T(1024)} %param.9) | copy-start | bytes 73732
Sparse Core Ops, SparseCore 0:
  10.8 58.3 all-gather.8
  71.5 139.0 all-gather.4
  213.4 56.7 all-gather.6
  272.9 54.5 all-gather.10
  370.8 139.2 reduce-scatter.4
  514.6 115.4 reduce-scatter.6
where the time goes:
time: 640 us; the launch traced here: 639 us
  waiting for transfers between devices  528 us (82%)
  matrix products  62.3 us (10%)
  local copies, waits for them, and re-layouts  20.1 us (3%)
  between operations  14.4 us (2%)
  other arithmetic  13.8 us (2%)
    all_gather x1, waiting for transfers between devices, per_device(): lax.all_gather(normed_own.astype(jnp.bfloat16), 'mp', axis=0, tiled=True)  141 us
    unnamed x7, waiting for transfers between devices  118 us
    reduce_scatter x1, waiting for transfers between devices, per_device(): lax.psum_scatter(running.astype(jnp.bfloat16), 'mp', scatter_dimension=0,...  110 us
    all_gather x1, waiting for transfers between devices, per_device(): lax.all_gather(w_query, 'dp', axis=0, tiled=True)  54.4 us
    all_gather x1, waiting for transfers between devices, per_device(): lax.all_gather(w_key, 'dp', axis=0, tiled=True)  53 us
    all_gather x1, waiting for transfers between devices, per_device(): lax.all_gather(w_value, 'dp', axis=0, tiled=True)  50.6 us
    dot_general x3, matrix products, per_device(): lax.dot_general(grad_item, weight_item, (((1,), (1,)), ((), ())), preferr...  27 us
    unnamed x25, local copies, waits for them, and re-layouts  13.6 us
  transfers between devices with their start and end apart: 6, of which 6 were waited for; matrix products, arithmetic and copies ran while one was open for 8% of the time, Pallas kernels for 0%

commit v1 on v0

v1 whole, which is shorter than its diff:
```python
import jax
import jax.numpy as jnp
from jax import lax
from jax.experimental import pallas as pl
from jax.experimental.pallas import tpu as pltpu
from jax.sharding import PartitionSpec as P

MESH = pl.DeviceIdType.MESH
F32 = jnp.float32
BF16 = jnp.bfloat16
NZ, NY = 8, 4
EPS = 1e-06

NAMES = (
    ["x0", "x1"]
    + [f"{n}{k}" for n in ("af", "hf", "xf") for k in (1, 2, 3, 4)]
    + [f"{n}{k}" for n in ("ab", "hb", "xb") for k in (1, 2, 3)]
    + ["wx"]
    + [f"{n}{k}" for n in ("wf1", "wf2", "wb1", "ws0", "wsf1", "wsf2", "wsb1") for k in (0, 1)]
    + [f"px{k}" for k in range(9)]
    + [f"{n}{k}" for n in ("paf", "phf") for k in (1, 2, 3, 4)]
    + [f"{n}{k}" for n in ("pab", "phb") for k in (1, 2, 3)]
    + [f"gs{k}" for k in range(8)]
    + [f"gy{k}" for k in range(6)]
    + ["gx"]
)
ID = {name: i for i, name in enumerate(NAMES)}


def dot(a, b, contract):
    return lax.dot_general(a, b, (contract, ((), ())), preferred_element_type=F32)


def unit(rows):
    centred = rows - jnp.mean(rows, axis=-1, keepdims=True)
    inv = lax.rsqrt(jnp.mean(centred * centred, axis=-1, keepdims=True) + EPS)
    return centred * inv, inv


def unit_back(grad, rows_unit, inv, gain):
    e = grad * gain
    inner = jnp.mean(e * rows_unit, axis=-1, keepdims=True)
    return (e - jnp.mean(e, axis=-1, keepdims=True) - rows_unit * inner) * inv


def kernel(
    tok, gain, qg, kg, wq, wk, wv, gh,
    out_tok, out_q, out_k, out_v,
    nrm, wts, part, gwt, rz, rx, rs, ry, rh, acc, grd, grt, go, send, recv, local,
):
    d, m = lax.axis_index("dp"), lax.axis_index("mp")
    core, y, xh = lax.rem(d, 2), lax.rem(d // 2, NY), d // (2 * NY)
    z, xl = m // 2, lax.rem(m, 2)
    s = 1 - 2 * core

    def zo(o):
        return lax.rem(z + o * s + NZ, NZ)

    def yo(o):
        return lax.rem(y + o * s + NY, NY)

    def dp(x_other, yy, c=core):
        return ((lax.rem(xh + x_other, 2)) * NY + yy) * 2 + c

    to_zf, to_zb, to_x = (d, zo(1) * 2 + xl), (d, zo(-1) * 2 + xl), (d, z * 2 + 1 - xl)
    to_yf, to_yb = (dp(0, yo(1)), m), (dp(0, yo(-1)), m)
    to_s, to_h = (dp(0, y, 1 - core), m), (dp(1, y), m)
    started = []

    def put(name, src, dst, device, land=None):
        copy = pltpu.make_async_remote_copy(
            src_ref=src, dst_ref=dst, send_sem=send.at[ID[name]], recv_sem=recv.at[ID[land or name]],
            device_id=device, device_id_type=MESH,
        )
        copy.start()
        started.append(copy)

    def got(name, dst):
        pltpu.make_async_remote_copy(
            src_ref=dst, dst_ref=dst, send_sem=send.at[ID[name]], recv_sem=recv.at[ID[name]],
            device_id=to_s, device_id_type=MESH,
        ).wait_recv()

    own = [
        pltpu.make_async_copy(w, wts.at[d, :, pl.ds(256 * i, 256)], local.at[i])
        for i, w in enumerate((wq, wk, wv))
    ]
    for copy in own:
        copy.start()
    heads_in = pltpu.make_async_copy(gh, go, local.at[3])
    heads_in.start()

    barrier = pltpu.get_barrier_semaphore()
    for device in (to_zf, to_zb, to_x, to_yf, to_yb, to_s, to_h):
        pl.semaphore_signal(barrier, inc=1, device_id=device, device_id_type=MESH)

    rows, _ = unit(tok[...].astype(F32))
    normed = (rows * gain[...]).astype(BF16)
    nrm[z, 0, xl] = normed[:16]
    nrm[z, 1, xl] = normed[16:]
    pl.semaphore_wait(barrier, 7)

    put("x0", nrm.at[z, 0, xl], nrm.at[z, 0, xl], to_x)
    put("af1", nrm.at[z, 1, xl], nrm.at[z, 1, xl], to_zf)
    put("ab1", nrm.at[z, 1, xl], nrm.at[z, 1, xl], to_zb)
    for copy in own:
        copy.wait()

    def put_w(name, block, device):
        put(name, wts.at[block], wts.at[block], device)

    put_w("wx", d, to_h)
    put_w("wf10", d, to_yf)
    put_w("wb10", d, to_yb)
    put_w("ws00", d, to_s)
    put("x1", nrm.at[z, 1, xl], nrm.at[z, 1, xl], to_x)

    def tokens_a(k, back):
        zz = zo(k) if back else zo(-k)
        block = nrm.at[zz, 1, xl]
        got(f"a{'b' if back else 'f'}{k}", block)
        if back and k < 3:
            put(f"ab{k + 1}", block, block, to_zb)
        if not back and k < 4:
            put(f"af{k + 1}", block, block, to_zf)
        put(f"x{'b' if back else 'f'}{k}", block, block, to_x)

    def tokens_h(k, back):
        zz = zo(k) if back else zo(-k)
        block = nrm.at[zz, 0]
        got(f"h{'b' if back else 'f'}{k}", block)
        if back and k < 3:
            put(f"hb{k + 1}", block, block, to_zb)
        if not back and k < 4:
            put(f"hf{k + 1}", block, block, to_zf)

    def weights(kind, x):
        block = dp(x, yo({"f1": -1, "f2": -2, "b1": 1}[kind]))
        got(f"w{kind}{x}", wts.at[block])
        if kind == "f1":
            put_w(f"wf2{x}", block, to_yf)
        put_w(f"ws{kind}{x}", block, to_s)

    got("x0", nrm.at[z, 0, 1 - xl])
    put("hf1", nrm.at[z, 0], nrm.at[z, 0], to_zf)
    put("hb1", nrm.at[z, 0], nrm.at[z, 0], to_zb)
    tokens_a(1, False)
    tokens_a(1, True)
    other = dp(1, y)
    got("wx", wts.at[other])
    put_w("wf11", other, to_yf)
    put_w("wb11", other, to_yb)
    put_w("ws01", other, to_s)
    weights("f1", 0)
    weights("b1", 0)
    tokens_h(1, False)
    tokens_h(1, True)
    tokens_a(2, False)
    tokens_a(2, True)
    weights("f1", 1)
    weights("b1", 1)
    tokens_h(2, False)
    tokens_h(2, True)
    tokens_a(3, False)
    tokens_a(3, True)
    weights("f2", 0)
    tokens_h(3, False)
    tokens_h(3, True)
    tokens_a(4, False)
    weights("f2", 1)
    tokens_h(4, False)
    got("x1", nrm.at[z, 1, 1 - xl])
    for k in (1, 2, 3, 4):
        got(f"xf{k}", nrm.at[zo(-k), 1, 1 - xl])
    for k in (1, 2, 3):
        got(f"xb{k}", nrm.at[zo(k), 1, 1 - xl])
    for x in (0, 1):
        got(f"ws0{x}", wts.at[dp(x, y, 1 - core)])
        got(f"wsf1{x}", wts.at[dp(x, yo(1), 1 - core)])
        got(f"wsb1{x}", wts.at[dp(x, yo(-1), 1 - core)])
        got(f"wsf2{x}", wts.at[dp(x, yo(2), 1 - core)])

    def columns(j):
        start = pl.multiple_of(j * 768, 768)
        return nrm[:, :, :, :, pl.ds(start, 768)].reshape(512, 768)

    acc[...] = dot(columns(0), wts[0:2].reshape(768, 768), ((1,), (0,)))

    @pl.loop(1, 8)
    def _(j):
        acc[...] += dot(columns(j), wts[pl.ds(2 * j, 2)].reshape(768, 768), ((1,), (0,)))

    heads_in.wait()
    q_gain, k_gain = qg[...], kg[...]

    @pl.loop(0, 2)
    def _(image):
        r = pl.ds(pl.multiple_of(image * 256, 256), 256)
        for h in (0, 1):
            q_unit, q_inv = unit(acc[r, h * 128 : h * 128 + 128])
            k_unit, k_inv = unit(acc[r, 256 + h * 128 : 384 + h * 128])
            value = acc[r, 512 + h * 128 : 640 + h * 128].astype(BF16)
            qn, kn = (q_unit * q_gain).astype(BF16), (k_unit * k_gain).astype(BF16)
            cot = go[r, h * 128 : h * 128 + 128]
            cot = jnp.concatenate(
                [cot[64 * a + 32 * c + 16 * b :][:16] for a in range(4) for b in range(2) for c in range(2)],
                axis=0,
            )
            scores = dot(qn, kn, ((1,), (1,))) * (128**-0.5)
            e = jnp.exp(scores - jnp.max(scores, axis=-1, keepdims=True))
            att = e / jnp.sum(e, axis=-1, keepdims=True)
            grad_v = dot(att.astype(BF16), cot, ((0,), (0,)))
            grad_p = dot(cot, value, ((1,), (1,)))
            delta = jnp.sum(att * grad_p, axis=-1, keepdims=True)
            grad_s = (att * (grad_p - delta) * (128**-0.5)).astype(BF16)
            grad_q = unit_back(dot(grad_s, kn, ((1,), (0,))), q_unit, q_inv, q_gain)
            grad_k = unit_back(dot(grad_s, qn, ((0,), (0,))), k_unit, k_inv, k_gain)
            for i, g in enumerate((grad_q, grad_k, grad_v)):
                c0 = i * 256 + h * 128
                grd[pl.ds(image * 4, 4), :, c0 : c0 + 128] = g.astype(BF16).reshape(4, 64, 128)
                grt[c0 : c0 + 128, r] = g.T.astype(BF16)

    def make_part(o1, o2):
        left = jnp.concatenate([grd[zo(o1)], grd[zo(o2)]], axis=0)

        @pl.loop(0, 8)
        def _(j):
            cols = pl.ds(pl.multiple_of(j * 768, 768), 768)
            p = dot(left, wts[pl.ds(2 * j, 2)].reshape(768, 768), ((1,), (1,))).astype(BF16)
            part[zo(o1), :, :, :, cols] = p[:64].reshape(2, 2, 16, 768)
            part[zo(o2), :, :, :, cols] = p[64:].reshape(2, 2, 16, 768)

        for o in (o1, o2):
            put(f"px{o % 8}", part.at[zo(o), 1, 1 - xl], rx.at[o % 8], to_x)

    def make_gw(o, x):
        j = lax.rem(xh + x, 2) * NY + yo(o)
        right = columns(j)

        @pl.loop(0, 3)
        def _(i):
            r = pl.ds(pl.multiple_of(i * 256, 256), 256)
            p = dot(grt[r, :], right, ((1,), (0,))).astype(BF16)
            gwt[2 * j, r, :] = p[:, :384]
            gwt[2 * j + 1, r, :] = p[:, 384:]

        there = (-o % 4) * 2 + x
        put(f"gs{(o % 4) * 2 + x}", gwt.at[2 * j + 1 - core], rs.at[there], to_s, f"gs{there}")

    def add(dst, *terms):
        total = dst[...].astype(F32)
        for t in terms:
            total = total + t[...].astype(F32)
        dst[...] = total.astype(BF16)

    def add_gw(o, x, y_names):
        block = gwt.at[dp(x, yo(o))]
        slot = (o % 4) * 2 + x
        got(f"gs{slot}", rs.at[slot])
        for n in y_names:
            got(f"gy{n}", ry.at[n])

        @pl.loop(0, 3)
        def _(i):
            r = pl.ds(pl.multiple_of(i * 256, 256), 256)
            add(block.at[r], rs.at[slot, r], *[ry.at[n, r] for n in y_names])

        return block

    def chain_a(o, slot):
        block = part.at[zo(o), 1, xl]
        got(f"px{o % 8}", rx.at[o % 8])
        terms = [rx.at[o % 8]]
        if slot is not None:
            got(("paf%d" % (slot + 1)) if slot < 4 else ("pab%d" % (slot - 3)), rz.at[slot, 2])
            terms.append(rz.at[slot, 2])
        add(block, *terms)
        if o > 0:
            put(f"paf{5 - o}", block, rz.at[4 - o, 2], to_zf)
        else:
            put(f"pab{4 + o}", block, rz.at[7 + o, 2], to_zb)

    def chain_h(o, slot):
        block = part.at[zo(o), 0]
        if slot is not None:
            got(("phf%d" % (slot + 1)) if slot < 4 else ("phb%d" % (slot - 3)), rz.at[slot, pl.ds(0, 2)])
            add(block, rz.at[slot, pl.ds(0, 2)])
        if o > 0:
            put(f"phf{5 - o}", block, rz.at[4 - o, pl.ds(0, 2)], to_zf)
        else:
            put(f"phb{4 + o}", block, rz.at[7 + o, pl.ds(0, 2)], to_zb)

    make_part(4, 3)
    chain_h(4, None)
    make_gw(2, 1)
    make_gw(2, 0)
    chain_a(4, None)
    make_part(-3, 2)
    chain_h(-3, None)
    make_gw(1, 1)
    make_gw(-1, 1)
    put("gy1", add_gw(2, 1, ()), ry.at[1], to_yf)
    put("gy0", add_gw(2, 0, ()), ry.at[0], to_yf)
    chain_a(-3, None)
    make_gw(1, 0)
    make_gw(-1, 0)
    put("gy5", add_gw(-1, 1, ()), ry.at[5], to_yb)
    chain_h(3, 0)
    chain_a(3, 0)
    make_part(-2, 1)
    put("gy4", add_gw(-1, 0, ()), ry.at[4], to_yb)
    chain_h(-2, 4)
    chain_a(-2, 4)
    make_gw(0, 1)
    make_gw(0, 0)
    put("gy3", add_gw(1, 1, (1,)), ry.at[3], to_yf)
    make_part(-1, 0)
    put("gy2", add_gw(1, 0, (0,)), ry.at[2], to_yf)
    chain_h(2, 1)
    chain_a(2, 1)
    chain_h(-1, 5)
    chain_a(-1, 5)
    put("gx", add_gw(0, 1, (3, 5)), rh, to_h)
    chain_h(1, 2)
    chain_a(1, 2)

    got("phb3", rz.at[6, pl.ds(0, 2)])
    got("phf4", rz.at[3, pl.ds(0, 2)])
    add(part.at[z, 0, 1 - xl], rz.at[6, 1 - xl], rz.at[3, 1 - xl])
    put("px8", part.at[z, 0, 1 - xl], rx.at[8], to_x)

    slot = 0
    got("gs0", rs.at[0])
    got("gy2", ry.at[2])
    got("gy4", ry.at[4])
    got("gx", rh)
    for i, out in enumerate((out_q, out_k, out_v)):
        r = pl.ds(256 * i, 256)
        total = gwt[d, r].astype(F32) + rs[slot, r].astype(F32)
        total += ry[2, r].astype(F32) + ry[4, r].astype(F32) + rh[r].astype(F32)
        out[...] = total.T.astype(BF16)

    got("px0", rx.at[0])
    got("pab3", rz.at[6, 2])
    got("paf4", rz.at[3, 2])
    got("px8", rx.at[8])
    half0 = part[z, 0, xl].astype(F32) + rz[6, xl].astype(F32) + rz[3, xl].astype(F32) + rx[8].astype(F32)
    half1 = part[z, 1, xl].astype(F32) + rz[6, 2].astype(F32) + rz[3, 2].astype(F32) + rx[0].astype(F32)
    for i, grad in enumerate((half0, half1)):
        rows, inv = unit(tok[16 * i : 16 * i + 16, :].astype(F32))
        out_tok[16 * i : 16 * i + 16, :] = unit_back(grad, rows, inv, gain[...]).astype(BF16)

    for copy in started:
        copy.wait_send()


def per_device(tokens, norm_gain, q_gain, k_gain, w_query, w_key, w_value, grad_heads):
    vmem, anywhere = pl.BlockSpec(memory_space=pltpu.VMEM), pl.BlockSpec(memory_space=pl.ANY)
    count = len(NAMES)
    return pl.pallas_call(
        kernel,
        out_shape=[
            jax.ShapeDtypeStruct(tokens.shape, BF16),
            jax.ShapeDtypeStruct(w_query.shape, BF16),
            jax.ShapeDtypeStruct(w_key.shape, BF16),
            jax.ShapeDtypeStruct(w_value.shape, BF16),
        ],
        in_specs=[vmem] * 4 + [anywhere] * 4,
        out_specs=[vmem] * 4,
        scratch_shapes=[
            pltpu.VMEM((8, 2, 2, 16, 6144), BF16),
            pltpu.VMEM((16, 384, 768), BF16),
            pltpu.VMEM((8, 2, 2, 16, 6144), BF16),
            pltpu.VMEM((16, 768, 384), BF16),
            pltpu.VMEM((7, 3, 16, 6144), BF16),
            pltpu.VMEM((9, 16, 6144), BF16),
            pltpu.VMEM((8, 768, 384), BF16),
            pltpu.VMEM((6, 768, 384), BF16),
            pltpu.VMEM((768, 384), BF16),
            pltpu.VMEM((512, 768), F32),
            pltpu.VMEM((8, 64, 768), BF16),
            pltpu.VMEM((768, 512), BF16),
            pltpu.VMEM((512, 256), BF16),
            pltpu.SemaphoreType.DMA((count,)),
            pltpu.SemaphoreType.DMA((count,)),
            pltpu.SemaphoreType.DMA((4,)),
        ],
        compiler_params=pltpu.CompilerParams(
            collective_id=0, has_side_effects=True, vmem_limit_bytes=64 * 1024 * 1024 - 65536
        ),
        cost_estimate=pl.CostEstimate(flops=15_000_000_000, bytes_accessed=3_000_000, transcendentals=300_000),
        name="attention_branch_back",
    )(
        tokens, norm_gain.reshape(1, -1), q_gain.reshape(1, -1), k_gain.reshape(1, -1),
        w_query, w_key, w_value, grad_heads,
    )


def solution(mesh):
    placed = (
        P(("dp", "mp"), None),
        P(),
        P(),
        P(),
        P("dp", "mp"),
        P("dp", "mp"),
        P("dp", "mp"),
        P("dp", "mp"),
    )
    return jax.shard_map(
        per_device,
        mesh=mesh,
        in_specs=placed,
        out_specs=(P(("dp", "mp"), None), P("dp", "mp"), P("dp", "mp"), P("dp", "mp")),
        check_vma=False,
    )
```

time: 640 us -> 146 us (0.23)
  waiting for transfers between devices: 528 us -> 0 us
  Pallas kernels: 0 us -> 140 us
  matrix products: 62.3 us -> 0 us
  local copies, waits for them, and re-layouts: 20.1 us -> 4.48 us
  other arithmetic: 13.8 us -> 0 us
  between operations: 14.4 us -> 0.65 us
    all_gather x4 -> x0, waiting for transfers between devices: 300 us -> none  [the longest x1 141 us: per_device(): lax.all_gather(normed_own.astype(jnp.bfloat16), 'mp', axis=0, tiled=True)]
    pallas_call x0 -> x1, Pallas kernels: none -> 140 us  [per_device(): pl.pallas_call(kernel, out_shape=[jax.ShapeDtypeStruct(tokens.shape, BF16...]
    unnamed x7 -> x0, waiting for transfers between devices: 118 us -> none
    reduce_scatter x1 -> x0, waiting for transfers between devices: 110 us -> none  [per_device(): lax.psum_scatter(running.astype(jnp.bfloat16), 'mp', scatter_dimension=0,...]
    dot_general x13 -> x0, matrix products: 60.8 us -> none  [the longest x3 27 us: per_device(): lax.dot_general(grad_item, weight_item, (((1,), (1,)), ((), ())), preferr...]
    unnamed x25 -> x10, local copies, waits for them, and re-layouts: 13.6 us -> 4.48 us
  transfers between devices with their start and end apart: 6 -> 0, of which waited for: 6 -> 0; matrix products, arithmetic and copies ran while one was open for 8% -> 0% of each run, Pallas kernels for 0% -> 0%
where the time goes in v1:
time: 146 us; the launch traced here: 145 us
  Pallas kernels  140 us (96%)
  local copies, waits for them, and re-layouts  4.48 us (3%)
    pallas_call x1, Pallas kernels, per_device(): pl.pallas_call(kernel, out_shape=[jax.ShapeDtypeStruct(tokens.shape, BF16...  140 us
    unnamed x10, local copies, waits for them, and re-layouts  4.48 us

profile of v1, /device:TPU:32, one launch (start us, length us, event | category | flops | bytes accessed | tf_op | source)
XLA Modules:
  0.0 145.2 jit_solution(415552604246920790)
XLA Ops:
  0.6 140.1 %attention_branch_back.1 = (bf16[32,6144]{1,0:T(8,128)(2,1)}, bf16[384,256]{1,0:T(8,128)(2,1)}, bf16[384,256]{1,0:T(8,128)(2,1)}, bf16[384,256]{1,0:T(8,128)(2,1)}) custom-call(bf16[32,6144]{1,0:T(8,128)(2,1)} %tok.1, f32[1,6144]{1,0:T(1,128)} %bitcast.3, f32[1,128]{1,0:T(1,128)} %bitcast.4, f32[1,128]{1,0:T(1,128)} %bitcast.5, bf16[384,256]{1,0:T(8,128)(2,1)} %wq.1, ...), custom_call_target="tpu_custom_call" | custom-call | flops 15000000512 | bytes 3000000 | tf_op jit(solution)/shard_map/attention_branch_back/pallas_call | solution.py:360
  140.7 0.0 copy-start.2
  140.7 1.8 %copy.16 = bf16[32,6144]{1,0:T(8,128)(2,1)} copy(bf16[32,6144]{1,0:T(8,128)(2,1)} %get-tuple-element.8) | data formatting | bytes 786432
  142.5 0.0 copy-done.2
  142.5 0.0 copy-start.1
  142.5 0.7 copy.17
  143.2 0.3 copy-done.1
  143.5 0.0 copy-start
  143.5 0.7 copy.18
  144.2 0.3 copy-done
  144.5 0.7 copy.19
Async XLA Ops:
  140.7 1.8 %copy-start.2 = (bf16[384,256]{1,0:T(8,128)(2,1)S(1)}, bf16[384,256]{1,0:T(8,128)(2,1)}, u32[]{:S(2)}) copy-start(bf16[384,256]{1,0:T(8,128)(2,1)} %get-tuple-element.9) | copy-start | bytes 589828
  142.5 1.0 copy-start.1
  143.5 1.0 copy-start

commit v2 on v1

v2 whole, which is shorter than its diff:
```python
import jax
import jax.numpy as jnp
from jax import lax
from jax.experimental import pallas as pl
from jax.experimental.pallas import tpu as pltpu
from jax.sharding import PartitionSpec as P

MESH = pl.DeviceIdType.MESH
F32 = jnp.float32
BF16 = jnp.bfloat16
NZ, NY = 8, 4
EPS = 1e-06

SPAN = {"A0": (0, 1536), "A1": (1536, 2688), "H0": (2688, 4992), "H1": (4992, 6144)}
A_COLS, H_COLS = 2688, 3456
STEPS = [("f", k) for k in (1, 2, 3, 4)] + [("b", k) for k in (1, 2, 3)]

NAMES = (
    [f"xo{g}" for g in SPAN]
    + [f"{t}{g}{w}{k}" for t in ("t", "p") for g in SPAN for w, k in STEPS]
    + [f"x{g}{w}{k}" for g in ("A0", "A1") for w, k in STEPS]
    + ["wx"]
    + [f"{n}{k}" for n in ("wf1", "wf2", "wb1", "ws0", "wsf1", "wsf2", "wsb1") for k in (0, 1)]
    + [f"px{g}{k}" for g in ("A0", "A1") for k in range(8)]
    + ["fxH0", "fxH1"]
    + [f"gs{k}" for k in range(8)]
    + [f"gy{k}" for k in range(6)]
    + ["gx"]
)
ID = {name: i for i, name in enumerate(NAMES)}

GATHER = (
    "A0f1", "A0b1", "A1f1", "oH0", "A1b1", "oH1", "A0f2", "A0b2",
    "A1f2", "wf10", "H0f1", "H0b1", "wb10", "A1b2", "H1f1", "H1b1",
    "wx", "A0f3", "A0b3", "wf20", "A1f3", "H0f2", "wf11", "H0b2",
    "A1b3", "H1f2", "H1b2", "A0f4", "A1f4", "wb11", "H0f3", "H0b3",
    "wf21", "H1f3", "H1b3", "H0f4", "H1f4",
)
SUM = (
    "PH1", "PA1", "G21", "H1f1", "G31", "G11", "A1f0", "H1b1",
    "PH0", "D21", "A1b0", "A1f1", "H1f2", "H1b2", "PA0", "G01",
    "D31", "H0f1", "G20", "G00", "H0b1", "G30", "D11", "A0f0",
    "A1f2", "A1b1", "G10", "A0b0", "H1f3", "H0f2", "D20", "H0b2",
    "A0f1", "A1f3", "D01", "A0b1", "A1b2", "H1pre", "D30", "H0f3",
    "D10", "A0f2", "A0b2", "A1fin", "H0pre", "A0f3", "H1fin", "D00",
    "A0fin", "H0fin",
)


def dot(a, b, contract):
    return lax.dot_general(a, b, (contract, ((), ())), preferred_element_type=F32)


def unit(rows):
    centred = rows - jnp.mean(rows, axis=-1, keepdims=True)
    inv = lax.rsqrt(jnp.mean(centred * centred, axis=-1, keepdims=True) + EPS)
    return centred * inv, inv


def unit_back(grad, rows_unit, inv, gain):
    e = grad * gain
    inner = jnp.mean(e * rows_unit, axis=-1, keepdims=True)
    return (e - jnp.mean(e, axis=-1, keepdims=True) - rows_unit * inner) * inv


def kernel(
    tok_in, gain, qg, kg, wq, wk, wv, gh,
    out_tok, out_q, out_k, out_v,
    tok, nrm, wts, part, gwt, rzh, rza, rxa, rxh, rs, ry, rh, acc, grd, grt, go, gsum, send, recv, local,
):
    d, m = lax.axis_index("dp"), lax.axis_index("mp")
    core, y, xh = lax.rem(d, 2), lax.rem(d // 2, NY), d // (2 * NY)
    z, xl = m // 2, lax.rem(m, 2)
    s = 1 - 2 * core

    def zo(o):
        return lax.rem(z + o * s + NZ, NZ)

    def yo(o):
        return lax.rem(y + o * s + NY, NY)

    def dp(x_other, yy, c=core):
        return ((lax.rem(xh + x_other, 2)) * NY + yy) * 2 + c

    to_zf, to_zb, to_x = (d, zo(1) * 2 + xl), (d, zo(-1) * 2 + xl), (d, z * 2 + 1 - xl)
    to_yf, to_yb = (dp(0, yo(1)), m), (dp(0, yo(-1)), m)
    to_s, to_h = (dp(0, y, 1 - core), m), (dp(1, y), m)
    started = []

    def put(name, src, dst, device, land=None):
        copy = pltpu.make_async_remote_copy(
            src_ref=src, dst_ref=dst, send_sem=send.at[ID[name]], recv_sem=recv.at[ID[land or name]],
            device_id=device, device_id_type=MESH,
        )
        copy.start()
        started.append(copy)

    def got(name, dst):
        pltpu.make_async_remote_copy(
            src_ref=dst, dst_ref=dst, send_sem=send.at[ID[name]], recv_sem=recv.at[ID[name]],
            device_id=to_s, device_id_type=MESH,
        ).wait_recv()

    tok_copy = pltpu.make_async_copy(tok_in, tok, local.at[4])
    tok_copy.start()
    own = [
        pltpu.make_async_copy(w, wts.at[d, :, pl.ds(256 * i, 256)], local.at[i])
        for i, w in enumerate((wq, wk, wv))
    ]
    for copy in own:
        copy.start()
    heads_in = pltpu.make_async_copy(gh, go, local.at[3])
    heads_in.start()

    barrier = pltpu.get_barrier_semaphore()
    for device in (to_zf, to_zb, to_x, to_yf, to_yb, to_s, to_h):
        pl.semaphore_signal(barrier, inc=1, device_id=device, device_id_type=MESH)

    tok_copy.wait()
    rows, _ = unit(tok[...].astype(F32))
    nrm[z, xl] = (rows * gain[...]).astype(BF16)
    pl.semaphore_wait(barrier, 7)

    def span(g):
        return pl.ds(SPAN[g][0], SPAN[g][1] - SPAN[g][0])

    def tokens_at(g, zz):
        return nrm.at[zz, xl, :, span(g)] if g[0] == "A" else nrm.at[zz, :, :, span(g)]

    def put_same(name, block, device):
        put(name, block, block, device)

    def put_w(name, block, device):
        put(name, wts.at[block], wts.at[block], device)

    def put_x(g):
        put_same(f"xo{g}", nrm.at[z, xl, :, span(g)], to_x)

    def put_z(g):
        put_same(f"t{g}f1", tokens_at(g, z), to_zf)
        put_same(f"t{g}b1", tokens_at(g, z), to_zb)

    def tokens_step(g, way, k):
        block = tokens_at(g, zo(-k if way == "f" else k))
        got(f"t{g}{way}{k}", block)
        if k < (4 if way == "f" else 3):
            put_same(f"t{g}{way}{k + 1}", block, to_zf if way == "f" else to_zb)
        if g[0] == "A":
            put_same(f"x{g}{way}{k}", block, to_x)

    def weights_step(kind, x):
        block = dp(x, yo({"f1": -1, "f2": -2, "b1": 1}[kind]))
        got(f"w{kind}{x}", wts.at[block])
        if kind == "f1":
            put_w(f"wf2{x}", block, to_yf)
        put_w(f"ws{kind}{x}", block, to_s)

    put_x("H0")
    put_z("A0")
    put_z("A1")
    for copy in own:
        copy.wait()
    put_w("wf10", d, to_yf)
    put_w("wb10", d, to_yb)
    put_x("H1")
    put_w("wx", d, to_h)
    put_w("ws00", d, to_s)
    put_x("A0")
    put_x("A1")
    for event in GATHER:
        if event[0] == "o":
            got(f"x{event}", nrm.at[z, 1 - xl, :, span(event[1:])])
            put_z(event[1:])
        elif event == "wx":
            block = dp(1, y)
            got("wx", wts.at[block])
            put_w("wf11", block, to_yf)
            put_w("wb11", block, to_yb)
            put_w("ws01", block, to_s)
        elif event[0] == "w":
            weights_step(event[1:3], int(event[3]))
        else:
            tokens_step(event[:2], event[2], int(event[3]))
    for g in ("A0", "A1"):
        got(f"xo{g}", nrm.at[z, 1 - xl, :, span(g)])
        for way, k in STEPS:
            got(f"x{g}{way}{k}", nrm.at[zo(-k if way == "f" else k), 1 - xl, :, span(g)])
    for x in (0, 1):
        got(f"ws0{x}", wts.at[dp(x, y, 1 - core)])
        got(f"wsf1{x}", wts.at[dp(x, yo(1), 1 - core)])
        got(f"wsb1{x}", wts.at[dp(x, yo(-1), 1 - core)])
        got(f"wsf2{x}", wts.at[dp(x, yo(2), 1 - core)])

    def columns(j):
        start = pl.multiple_of(j * 768, 768)
        return nrm[:, :, :, pl.ds(start, 768)].reshape(512, 768)

    acc[...] = dot(columns(0), wts[0:2].reshape(768, 768), ((1,), (0,)))

    @pl.loop(1, 8)
    def _(j):
        acc[...] += dot(columns(j), wts[pl.ds(2 * j, 2)].reshape(768, 768), ((1,), (0,)))

    heads_in.wait()
    q_gain, k_gain = qg[...], kg[...]

    for image in (0, 1):
        r = slice(image * 256, image * 256 + 256)
        for h in (0, 1):
            q_unit, q_inv = unit(acc[r, h * 128 : h * 128 + 128])
            k_unit, k_inv = unit(acc[r, 256 + h * 128 : 384 + h * 128])
            value = acc[r, 512 + h * 128 : 640 + h * 128].astype(BF16)
            qn, kn = (q_unit * q_gain).astype(BF16), (k_unit * k_gain).astype(BF16)
            cot = go[r, h * 128 : h * 128 + 128]
            scores = dot(qn, kn, ((1,), (1,))) * (128**-0.5)
            e = jnp.exp(scores - jnp.max(scores, axis=-1, keepdims=True))
            att = e / jnp.sum(e, axis=-1, keepdims=True)
            grad_v = dot(att.astype(BF16), cot, ((0,), (0,)))
            grad_p = dot(cot, value, ((1,), (1,)))
            delta = jnp.sum(att * grad_p, axis=-1, keepdims=True)
            grad_s = (att * (grad_p - delta) * (128**-0.5)).astype(BF16)
            grad_q = unit_back(dot(grad_s, kn, ((1,), (0,))), q_unit, q_inv, q_gain)
            grad_k = unit_back(dot(grad_s, qn, ((0,), (0,))), k_unit, k_inv, k_gain)
            for i, g in enumerate((grad_q, grad_k, grad_v)):
                c0 = i * 256 + h * 128
                grd[r, c0 : c0 + 128] = g.astype(BF16)
                grt[c0 : c0 + 128, r] = g.T.astype(BF16)

    offsets = (4, -3, 3, -2, 2, -1, 1, 0)

    def make_part(g):
        first, last = SPAN[g][0] // 384, SPAN[g][1] // 384
        blocks = 2 if (last - first) % 2 == 0 else last - first
        width = blocks * 384

        @pl.loop(0, (last - first) // blocks)
        def _(i):
            w = wts[pl.ds(first + i * blocks, blocks)].reshape(width, 768)
            cols = pl.ds(pl.multiple_of(SPAN[g][0] + i * width, 128), width)
            part[:, :, :, cols] = dot(grd[...], w, ((1,), (1,))).astype(BF16).reshape(8, 2, 32, width)

        if g[0] == "A":
            for o in offsets:
                put(f"px{g}{o % 8}", part.at[zo(o), 1 - xl, :, span(g)], rxa.at[o % 8, :, span(g)], to_x)
        else:
            chain(g, "f", 0)
            chain(g, "b", 0)

    def make_gw(o, x):
        j = lax.rem(xh + x, 2) * NY + yo(o)
        p = dot(grt[...], columns(j), ((1,), (0,))).astype(BF16)
        gwt[2 * j] = p[:, :384]
        gwt[2 * j + 1] = p[:, 384:]
        there = (-o % 4) * 2 + x
        put(f"gs{(o % 4) * 2 + x}", gwt.at[2 * j + 1 - core], rs.at[there], to_s, f"gs{there}")

    def add(dst, *terms):
        total = dst[...].astype(F32)
        for t in terms:
            total = total + t[...].astype(F32)
        dst[...] = total.astype(BF16)

    def landing(g, way, k):
        slot = k - 1 if way == "f" else 3 + k
        start, end = SPAN[g]
        if g[0] == "A":
            return rza.at[slot, :, pl.ds(start, end - start)]
        return rzh.at[slot, :, :, pl.ds(start - A_COLS, end - start)]

    def chain(g, way, k):
        o = 4 - k if way == "f" else k - 3
        block = part.at[zo(o), xl, :, span(g)] if g[0] == "A" else part.at[zo(o), :, :, span(g)]
        terms = []
        if g[0] == "A":
            got(f"px{g}{o % 8}", rxa.at[o % 8, :, span(g)])
            terms.append(rxa.at[o % 8, :, span(g)])
        if k > 0:
            got(f"p{g}{way}{k}", landing(g, way, k))
            terms.append(landing(g, way, k))
        if terms:
            add(block, *terms)
        put(f"p{g}{way}{k + 1}", block, landing(g, way, k + 1), to_zf if way == "f" else to_zb)

    def chain_end(g):
        got(f"p{g}b3", landing(g, "b", 3))
        got(f"p{g}f4", landing(g, "f", 4))
        if g[0] == "H":
            block = part.at[z, 1 - xl, :, span(g)]
            add(block, landing(g, "b", 3).at[1 - xl], landing(g, "f", 4).at[1 - xl])
            put(f"fx{g}", block, rxh.at[:, pl.ds(SPAN[g][0] - A_COLS, SPAN[g][1] - SPAN[g][0])], to_x)

    def finish_tokens(g):
        back, ahead = landing(g, "b", 3), landing(g, "f", 4)
        if g[0] == "A":
            chain_end(g)
            over = rxa.at[0, :, span(g)]
            got(f"px{g}0", over)
        else:
            back, ahead = back.at[xl], ahead.at[xl]
            over = rxh.at[:, pl.ds(SPAN[g][0] - A_COLS, SPAN[g][1] - SPAN[g][0])]
            got(f"fx{g}", over)
        total = part[z, xl, :, span(g)].astype(F32) + back[...].astype(F32)
        gsum[:, span(g)] = total + ahead[...].astype(F32) + over[...].astype(F32)

    def add_gw(o, x):
        slot = (o % 4) * 2 + x
        got(f"gs{slot}", rs.at[slot])
        arrivals = {1: (x,), 0: (2 + x, 4 + x)}.get(o, ())
        for n in arrivals:
            got(f"gy{n}", ry.at[n])
        if o == 0 and x == 0:
            got("gx", rh)
            for i, out in enumerate((out_q, out_k, out_v)):
                r = pl.ds(256 * i, 256)
                total = gwt[d, r].astype(F32) + rs[0, r].astype(F32)
                total += ry[2, r].astype(F32) + ry[4, r].astype(F32) + rh[r].astype(F32)
                out[...] = total.T.astype(BF16)
            return
        block = gwt.at[dp(x, yo(o))]

        @pl.loop(0, 3)
        def _(i):
            r = pl.ds(pl.multiple_of(i * 256, 256), 256)
            add(block.at[r], rs.at[slot, r], *[ry.at[n, r] for n in arrivals])

        if o == 0:
            put("gx", block, rh, to_h)
        else:
            n = {2: 0, 1: 2, -1: 4}[o] + x
            put(f"gy{n}", block, ry.at[n], to_yb if o == -1 else to_yf)

    for event in SUM:
        if event[0] == "P":
            make_part(event[1:])
        elif event[0] in "GD":
            (make_gw if event[0] == "G" else add_gw)({"3": -1}.get(event[1], int(event[1])), int(event[2]))
        elif event[2:] == "pre":
            chain_end(event[:2])
        elif event[2:] == "fin":
            finish_tokens(event[:2])
        else:
            chain(event[:2], event[2], int(event[3]))

    rows, inv = unit(tok[...].astype(F32))
    out_tok[...] = unit_back(gsum[...], rows, inv, gain[...]).astype(BF16)

    for copy in started:
        copy.wait_send()


def hand_on(*refs):
    ins, outs, sems = refs[:4], refs[4:8], refs[8]
    copies = [pltpu.make_async_copy(a, b, sems.at[i]) for i, (a, b) in enumerate(zip(ins, outs))]
    for copy in copies:
        copy.start()
    for copy in copies:
        copy.wait()


def per_device(tokens, norm_gain, q_gain, k_gain, w_query, w_key, w_value, grad_heads):
    vmem, anywhere = pl.BlockSpec(memory_space=pltpu.VMEM), pl.BlockSpec(memory_space=pl.ANY)
    count = len(NAMES)
    shapes = [jax.ShapeDtypeStruct(a.shape, BF16) for a in (tokens, w_query, w_key, w_value)]
    results = pl.pallas_call(
        kernel,
        out_shape=shapes,
        in_specs=[anywhere] + [vmem] * 3 + [anywhere] * 4,
        out_specs=[vmem] * 4,
        scratch_shapes=[
            pltpu.VMEM((32, 6144), BF16),
            pltpu.VMEM((8, 2, 32, 6144), BF16),
            pltpu.VMEM((16, 384, 768), BF16),
            pltpu.VMEM((8, 2, 32, 6144), BF16),
            pltpu.VMEM((16, 768, 384), BF16),
            pltpu.VMEM((7, 2, 32, H_COLS), BF16),
            pltpu.VMEM((7, 32, A_COLS), BF16),
            pltpu.VMEM((8, 32, A_COLS), BF16),
            pltpu.VMEM((32, H_COLS), BF16),
            pltpu.VMEM((8, 768, 384), BF16),
            pltpu.VMEM((6, 768, 384), BF16),
            pltpu.VMEM((768, 384), BF16),
            pltpu.VMEM((512, 768), F32),
            pltpu.VMEM((512, 768), BF16),
            pltpu.VMEM((768, 512), BF16),
            pltpu.VMEM((512, 256), BF16),
            pltpu.VMEM((32, 6144), F32),
            pltpu.SemaphoreType.DMA((count,)),
            pltpu.SemaphoreType.DMA((count,)),
            pltpu.SemaphoreType.DMA((5,)),
        ],
        compiler_params=pltpu.CompilerParams(
            collective_id=0, has_side_effects=True, vmem_limit_bytes=64 * 1024 * 1024 - 65536
        ),
        cost_estimate=pl.CostEstimate(flops=15_000_000_000, bytes_accessed=3_000_000, transcendentals=300_000),
        name="attention_branch_back",
    )(
        tokens, norm_gain.reshape(1, -1), q_gain.reshape(1, -1), k_gain.reshape(1, -1),
        w_query, w_key, w_value, grad_heads,
    )
    return pl.pallas_call(
        hand_on,
        out_shape=shapes,
        in_specs=[vmem] * 4,
        out_specs=[anywhere] * 4,
        scratch_shapes=[pltpu.SemaphoreType.DMA((4,))],
        name="hand_on",
    )(*results)


def solution(mesh):
    placed = (
        P(("dp", "mp"), None),
        P(),
        P(),
        P(),
        P("dp", "mp"),
        P("dp", "mp"),
        P("dp", "mp"),
        P("dp", "mp"),
    )
    return jax.shard_map(
        per_device,
        mesh=mesh,
        in_specs=placed,
        out_specs=(P(("dp", "mp"), None), P("dp", "mp"), P("dp", "mp"), P("dp", "mp")),
        check_vma=False,
    )
```

time: 146 us -> 133 us (0.911)
  Pallas kernels: 140 us -> 132 us
  local copies, waits for them, and re-layouts: 4.48 us -> 0 us
    pallas_call x1 -> x2, Pallas kernels: 140 us -> 132 us  [the longest x1 130 us: per_device(): pl.pallas_call(kernel, out_shape=shapes, in_specs=[anywhere] + [vmem] * 3...]
    unnamed x10 -> x0, local copies, waits for them, and re-layouts: 4.48 us -> none
where the time goes in v2:
time: 133 us
  Pallas kernels  132 us (99%)
    pallas_call x1, Pallas kernels, per_device(): pl.pallas_call(kernel, out_shape=shapes, in_specs=[anywhere] + [vmem] * 3...  130 us

profile of v2, /device:TPU:32, one launch (start us, length us, event | category | flops | bytes accessed | tf_op | source)
XLA Modules:
  0.0 133.0 jit_solution(9701516560811899970)
XLA Ops:
  0.6 130.0 %attention_branch_back.1 = (bf16[32,6144]{1,0:T(8,128)(2,1)}, bf16[384,256]{1,0:T(8,128)(2,1)}, bf16[384,256]{1,0:T(8,128)(2,1)}, bf16[384,256]{1,0:T(8,128)(2,1)}) custom-call(bf16[32,6144]{1,0:T(8,128)(2,1)} %tok_in.1, f32[1,6144]{1,0:T(1,128)} %bitcast.3, f32[1,128]{1,0:T(1,128)} %bitcast.4, f32[1,128]{1,0:T(1,128)} %bitcast.5, bf16[384,256]{1,0:T(8,128)(2,1)} %wq.1, ...), custom_call_target="tpu_custom_call" | custom-call | flops 15000000512 | bytes 3000000 | tf_op jit(solution)/shard_map/attention_branch_back/pallas_call | solution.py:364
  130.7 2.2 %hand_on.1 = (bf16[32,6144]{1,0:T(8,128)(2,1)}, bf16[384,256]{1,0:T(8,128)(2,1)}, bf16[384,256]{1,0:T(8,128)(2,1)}, bf16[384,256]{1,0:T(8,128)(2,1)}) custom-call(bf16[32,6144]{1,0:T(8,128)(2,1)} %get-tuple-element.8.refs_0_, bf16[384,256]{1,0:T(8,128)(2,1)} %get-tuple-element.9.refs_1_, bf16[384,256]{1,0:T(8,128)(2,1)} %get-tuple-element.10.refs_2_, ...), custom_call_target="tpu_custom_call" | custom-call | tf_op jit(solution)/shard_map/hand_on/pallas_call | solution.py:400

commit v3 on v2

--- a/solution.py
+++ b/solution.py
@@ -12,17 +12,19 @@
 EPS = 1e-06
 
 SPAN = {"A0": (0, 1536), "A1": (1536, 2688), "H0": (2688, 4992), "H1": (4992, 6144)}
+SUMS = {"A0": (0, 768), "A1": (768, 2688), "H0": (2688, 3840), "H1": (3840, 6144)}
 A_COLS, H_COLS = 2688, 3456
 STEPS = [("f", k) for k in (1, 2, 3, 4)] + [("b", k) for k in (1, 2, 3)]
 
 NAMES = (
     [f"xo{g}" for g in SPAN]
-    + [f"{t}{g}{w}{k}" for t in ("t", "p") for g in SPAN for w, k in STEPS]
+    + [f"t{g}{w}{k}" for g in SPAN for w, k in STEPS]
+    + [f"p{g}{w}{k}" for g in SUMS for w, k in STEPS]
     + [f"x{g}{w}{k}" for g in ("A0", "A1") for w, k in STEPS]
     + ["wx"]
     + [f"{n}{k}" for n in ("wf1", "wf2", "wb1", "ws0", "wsf1", "wsf2", "wsb1") for k in (0, 1)]
-    + [f"px{g}{k}" for g in ("A0", "A1") for k in range(8)]
-    + ["fxH0", "fxH1"]
+    + [f"px{g}{k}" for g in SUMS if g[0] == "A" for k in range(8)]
+    + [f"fx{g}" for g in SUMS if g[0] == "H"]
     + [f"gs{k}" for k in range(8)]
     + [f"gy{k}" for k in range(6)]
     + ["gx"]
@@ -37,13 +39,13 @@
     "wf21", "H1f3", "H1b3", "H0f4", "H1f4",
 )
 SUM = (
-    "PH1", "PA1", "G21", "H1f1", "G31", "G11", "A1f0", "H1b1",
-    "PH0", "D21", "A1b0", "A1f1", "H1f2", "H1b2", "PA0", "G01",
-    "D31", "H0f1", "G20", "G00", "H0b1", "G30", "D11", "A0f0",
-    "A1f2", "A1b1", "G10", "A0b0", "H1f3", "H0f2", "D20", "H0b2",
-    "A0f1", "A1f3", "D01", "A0b1", "A1b2", "H1pre", "D30", "H0f3",
-    "D10", "A0f2", "A0b2", "A1fin", "H0pre", "A0f3", "H1fin", "D00",
-    "A0fin", "H0fin",
+    "PH0", "PA0", "G21", "PH1", "A0f0", "A0b0", "H0f1", "H0b1",
+    "PA1", "D21", "G31", "H1f1", "G11", "G20", "G01", "G30",
+    "H1b1", "A0f1", "G00", "A0b1", "A1f0", "G10", "D31", "H0f2",
+    "A1b0", "H0b2", "D11", "H1f2", "D20", "H1b2", "A0f2", "A0b2",
+    "A1f1", "H0f3", "A1b1", "D01", "D30", "H1f3", "A0f3", "A1f2",
+    "D10", "H0pre", "A1b2", "H1pre", "A0fin", "H0fin", "A1f3", "D00",
+    "A1fin", "H1fin",
 )
 
 
@@ -195,11 +197,11 @@
         start = pl.multiple_of(j * 768, 768)
         return nrm[:, :, :, pl.ds(start, 768)].reshape(512, 768)
 
-    acc[...] = dot(columns(0), wts[0:2].reshape(768, 768), ((1,), (0,)))
-
-    @pl.loop(1, 8)
-    def _(j):
-        acc[...] += dot(columns(j), wts[pl.ds(2 * j, 2)].reshape(768, 768), ((1,), (0,)))
+    @pl.loop(0, 2)
+    def _(image):
+        rows = nrm[pl.ds(4 * image, 4)].reshape(256, 6144)
+        r = pl.ds(pl.multiple_of(256 * image, 256), 256)
+        acc[r] = dot(rows, wts[...].reshape(6144, 768), ((1,), (0,)))
 
     heads_in.wait()
     q_gain, k_gain = qg[...], kg[...]
@@ -226,22 +228,25 @@
                 grd[r, c0 : c0 + 128] = g.astype(BF16)
                 grt[c0 : c0 + 128, r] = g.T.astype(BF16)
 
+    def cols_of(g):
+        return pl.ds(SUMS[g][0], SUMS[g][1] - SUMS[g][0])
+
     offsets = (4, -3, 3, -2, 2, -1, 1, 0)
 
     def make_part(g):
-        first, last = SPAN[g][0] // 384, SPAN[g][1] // 384
+        first, last = SUMS[g][0] // 384, SUMS[g][1] // 384
         blocks = 2 if (last - first) % 2 == 0 else last - first
         width = blocks * 384
 
         @pl.loop(0, (last - first) // blocks)
         def _(i):
             w = wts[pl.ds(first + i * blocks, blocks)].reshape(width, 768)
-            cols = pl.ds(pl.multiple_of(SPAN[g][0] + i * width, 128), width)
+            cols = pl.ds(pl.multiple_of(SUMS[g][0] + i * width, 128), width)
             part[:, :, :, cols] = dot(grd[...], w, ((1,), (1,))).astype(BF16).reshape(8, 2, 32, width)
 
         if g[0] == "A":
             for o in offsets:
-                put(f"px{g}{o % 8}", part.at[zo(o), 1 - xl, :, span(g)], rxa.at[o % 8, :, span(g)], to_x)
+                put(f"px{g}{o % 8}", part.at[zo(o), 1 - xl, :, cols_of(g)], rxa.at[o % 8, :, cols_of(g)], to_x)
         else:
             chain(g, "f", 0)
             chain(g, "b", 0)
@@ -262,18 +267,18 @@
 
     def landing(g, way, k):
         slot = k - 1 if way == "f" else 3 + k
-        start, end = SPAN[g]
+        start, end = SUMS[g]
         if g[0] == "A":
             return rza.at[slot, :, pl.ds(start, end - start)]
         return rzh.at[slot, :, :, pl.ds(start - A_COLS, end - start)]
 
     def chain(g, way, k):
         o = 4 - k if way == "f" else k - 3
-        block = part.at[zo(o), xl, :, span(g)] if g[0] == "A" else part.at[zo(o), :, :, span(g)]
+        block = part.at[zo(o), xl, :, cols_of(g)] if g[0] == "A" else part.at[zo(o), :, :, cols_of(g)]
         terms = []
         if g[0] == "A":
-            got(f"px{g}{o % 8}", rxa.at[o % 8, :, span(g)])
-            terms.append(rxa.at[o % 8, :, span(g)])
+            got(f"px{g}{o % 8}", rxa.at[o % 8, :, cols_of(g)])
+            terms.append(rxa.at[o % 8, :, cols_of(g)])
         if k > 0:
             got(f"p{g}{way}{k}", landing(g, way, k))
             terms.append(landing(g, way, k))
@@ -285,22 +290,22 @@
         got(f"p{g}b3", landing(g, "b", 3))
         got(f"p{g}f4", landing(g, "f", 4))
         if g[0] == "H":
-            block = part.at[z, 1 - xl, :, span(g)]
+            block = part.at[z, 1 - xl, :, cols_of(g)]
             add(block, landing(g, "b", 3).at[1 - xl], landing(g, "f", 4).at[1 - xl])
-            put(f"fx{g}", block, rxh.at[:, pl.ds(SPAN[g][0] - A_COLS, SPAN[g][1] - SPAN[g][0])], to_x)
+            put(f"fx{g}", block, rxh.at[:, pl.ds(SUMS[g][0] - A_COLS, SUMS[g][1] - SUMS[g][0])], to_x)
 
     def finish_tokens(g):
         back, ahead = landing(g, "b", 3), landing(g, "f", 4)
         if g[0] == "A":
             chain_end(g)
-            over = rxa.at[0, :, span(g)]
+            over = rxa.at[0, :, cols_of(g)]
             got(f"px{g}0", over)
         else:
             back, ahead = back.at[xl], ahead.at[xl]
-            over = rxh.at[:, pl.ds(SPAN[g][0] - A_COLS, SPAN[g][1] - SPAN[g][0])]
+            over = rxh.at[:, pl.ds(SUMS[g][0] - A_COLS, SUMS[g][1] - SUMS[g][0])]
             got(f"fx{g}", over)
-        total = part[z, xl, :, span(g)].astype(F32) + back[...].astype(F32)
-        gsum[:, span(g)] = total + ahead[...].astype(F32) + over[...].astype(F32)
+        total = part[z, xl, :, cols_of(g)].astype(F32) + back[...].astype(F32)
+        gsum[:, cols_of(g)] = total + ahead[...].astype(F32) + over[...].astype(F32)
 
     def add_gw(o, x):
         slot = (o % 4) * 2 + x

time: 133 us -> 129 us (0.970)
  Pallas kernels: 132 us -> 127 us
    pallas_call x1, Pallas kernels: 130 us -> 125 us  [per_device(): pl.pallas_call(kernel, out_shape=shapes, in_specs=[anywhere] + [vmem] * 3...]
where the time goes in v3:
time: 129 us; the launch traced here: 128 us
  Pallas kernels  127 us (98%)
    pallas_call x1, Pallas kernels, per_device(): pl.pallas_call(kernel, out_shape=shapes, in_specs=[anywhere] + [vmem] * 3...  125 us

profile of v3, /device:TPU:32, one launch (start us, length us, event | category | flops | bytes accessed | tf_op | source)
XLA Modules:
  0.0 128.0 jit_solution(4629350901000156819)
XLA Ops:
  0.6 125.0 %attention_branch_back.1 = (bf16[32,6144]{1,0:T(8,128)(2,1)}, bf16[384,256]{1,0:T(8,128)(2,1)}, bf16[384,256]{1,0:T(8,128)(2,1)}, bf16[384,256]{1,0:T(8,128)(2,1)}) custom-call(bf16[32,6144]{1,0:T(8,128)(2,1)} %tok_in.1, f32[1,6144]{1,0:T(1,128)} %bitcast.3, f32[1,128]{1,0:T(1,128)} %bitcast.4, f32[1,128]{1,0:T(1,128)} %bitcast.5, bf16[384,256]{1,0:T(8,128)(2,1)} %wq.1, ...), custom_call_target="tpu_custom_call" | custom-call | flops 15000000512 | bytes 3000000 | tf_op jit(solution)/shard_map/attention_branch_back/pallas_call | solution.py:369
  125.6 2.2 %hand_on.1 = (bf16[32,6144]{1,0:T(8,128)(2,1)}, bf16[384,256]{1,0:T(8,128)(2,1)}, bf16[384,256]{1,0:T(8,128)(2,1)}, bf16[384,256]{1,0:T(8,128)(2,1)}) custom-call(bf16[32,6144]{1,0:T(8,128)(2,1)} %get-tuple-element.8.refs_0_, bf16[384,256]{1,0:T(8,128)(2,1)} %get-tuple-element.9.refs_1_, bf16[384,256]{1,0:T(8,128)(2,1)} %get-tuple-element.10.refs_2_, ...), custom_call_target="tpu_custom_call" | custom-call | tf_op jit(solution)/shard_map/hand_on/pallas_call | solution.py:405

commit v4 on v3

--- a/solution.py
+++ b/solution.py
@@ -35,17 +35,17 @@
     "A0f1", "A0b1", "A1f1", "oH0", "A1b1", "oH1", "A0f2", "A0b2",
     "A1f2", "wf10", "H0f1", "H0b1", "wb10", "A1b2", "H1f1", "H1b1",
     "wx", "A0f3", "A0b3", "wf20", "A1f3", "H0f2", "wf11", "H0b2",
-    "A1b3", "H1f2", "H1b2", "A0f4", "A1f4", "wb11", "H0f3", "H0b3",
-    "wf21", "H1f3", "H1b3", "H0f4", "H1f4",
+    "A1b3", "H1f2", "H1b2", "A0f4", "A1f4", "wb11", "near1", "H0f3", "H0b3",
+    "wf21", "H1f3", "H1b3", "near2", "H0f4", "H1f4",
 )
 SUM = (
     "PH0", "PA0", "G21", "PH1", "A0f0", "A0b0", "H0f1", "H0b1",
-    "PA1", "D21", "G31", "H1f1", "G11", "G20", "G01", "G30",
-    "H1b1", "A0f1", "G00", "A0b1", "A1f0", "G10", "D31", "H0f2",
-    "A1b0", "H0b2", "D11", "H1f2", "D20", "H1b2", "A0f2", "A0b2",
-    "A1f1", "H0f3", "A1b1", "D01", "D30", "H1f3", "A0f3", "A1f2",
-    "D10", "H0pre", "A1b2", "H1pre", "A0fin", "H0fin", "A1f3", "D00",
-    "A1fin", "H1fin",
+    "PA1", "D21", "G31", "G11", "G20", "H1f1", "G01", "G30",
+    "H1b1", "A0f1", "A0b1", "A1f0", "D31", "G00", "G10", "H0f2",
+    "A1b0", "H0b2", "D11", "D20", "H1f2", "D30", "H1b2", "A0f2",
+    "A0b2", "A1f1", "H0f3", "A1b1", "D01", "H1f3", "A0f3", "A1f2",
+    "A1b2", "H0pre", "D10", "H1pre", "A0fin", "H0fin", "A1f3", "A1fin",
+    "D00", "H1fin",
 )
 
 
@@ -156,6 +156,33 @@
         if kind == "f1":
             put_w(f"wf2{x}", block, to_yf)
         put_w(f"ws{kind}{x}", block, to_s)
+
+    def columns(j):
+        start = pl.multiple_of(j * 768, 768)
+        return nrm[:, :, :, pl.ds(start, 768)].reshape(512, 768)
+
+    def over_x(*ks):
+        for g in ("A0", "A1"):
+            for way, k in STEPS:
+                if k in ks:
+                    got(f"x{g}{way}{k}", nrm.at[zo(-k if way == "f" else k), 1 - xl, :, span(g)])
+
+    def project_near(chips, first=False):
+        for n, (x, o) in enumerate(chips):
+            j = lax.rem(xh + x, 2) * NY + yo(o)
+            cols = pl.ds(pl.multiple_of(j * 768, 768), 768)
+            left = [nrm[zo(q), :, :, cols].reshape(64, 768) for q in (0, 1, 2, -2, -1)]
+            p = dot(jnp.concatenate(left, axis=0), wts[pl.ds(2 * j, 2)].reshape(768, 768), ((1,), (0,)))
+            if first and n == 0:
+                acc[0:3] = p[:192].reshape(3, 64, 768)
+                acc[6:8] = p[192:].reshape(2, 64, 768)
+            else:
+                acc[0:3] += p[:192].reshape(3, 64, 768)
+                acc[6:8] += p[192:].reshape(2, 64, 768)
+
+    def sibling_weights(kinds, x):
+        for kind in kinds:
+            got(f"ws{kind}{x}", wts.at[dp(x, yo({"0": 0, "f1": 1, "b1": -1, "f2": 2}[kind]), 1 - core)])
 
     put_x("H0")
     put_z("A0")
@@ -170,7 +197,17 @@
     put_x("A0")
     put_x("A1")
     for event in GATHER:
-        if event[0] == "o":
+        if event == "near1":
+            for g in ("A0", "A1"):
+                got(f"xo{g}", nrm.at[z, 1 - xl, :, span(g)])
+            over_x(1, 2)
+            sibling_weights(("0", "f1", "b1", "f2"), 0)
+            sibling_weights(("0",), 1)
+            project_near(((0, 0), (0, 1), (0, -1), (1, 0), (0, 2)), first=True)
+        elif event == "near2":
+            sibling_weights(("f1", "b1"), 1)
+            project_near(((1, 1), (1, -1)))
+        elif event[0] == "o":
             got(f"x{event}", nrm.at[z, 1 - xl, :, span(event[1:])])
             put_z(event[1:])
         elif event == "wx":
@@ -183,35 +220,26 @@
             weights_step(event[1:3], int(event[3]))
         else:
             tokens_step(event[:2], event[2], int(event[3]))
-    for g in ("A0", "A1"):
-        got(f"xo{g}", nrm.at[z, 1 - xl, :, span(g)])
-        for way, k in STEPS:
-            got(f"x{g}{way}{k}", nrm.at[zo(-k if way == "f" else k), 1 - xl, :, span(g)])
-    for x in (0, 1):
-        got(f"ws0{x}", wts.at[dp(x, y, 1 - core)])
-        got(f"wsf1{x}", wts.at[dp(x, yo(1), 1 - core)])
-        got(f"wsb1{x}", wts.at[dp(x, yo(-1), 1 - core)])
-        got(f"wsf2{x}", wts.at[dp(x, yo(2), 1 - core)])
-
-    def columns(j):
-        start = pl.multiple_of(j * 768, 768)
-        return nrm[:, :, :, pl.ds(start, 768)].reshape(512, 768)
-
-    @pl.loop(0, 2)
-    def _(image):
-        rows = nrm[pl.ds(4 * image, 4)].reshape(256, 6144)
-        r = pl.ds(pl.multiple_of(256 * image, 256), 256)
-        acc[r] = dot(rows, wts[...].reshape(6144, 768), ((1,), (0,)))
+    over_x(3, 4)
+    got("wsf21", wts.at[dp(1, yo(2), 1 - core)])
+    far = jnp.concatenate([nrm[zo(q)].reshape(64, 6144) for q in (3, 4, -3)], axis=0)
+    acc[3:6] = dot(far, wts[...].reshape(6144, 768), ((1,), (0,))).reshape(3, 64, 768)
+    project_near(((1, 2),))
 
     heads_in.wait()
     q_gain, k_gain = qg[...], kg[...]
+
+    def projected(image, column):
+        places = [lax.rem((4 * image + i - z) * s + NZ, NZ) for i in range(4)]
+        return jnp.concatenate([acc[at, :, column : column + 128] for at in places], axis=0)
+
 
     for image in (0, 1):
         r = slice(image * 256, image * 256 + 256)
         for h in (0, 1):
-            q_unit, q_inv = unit(acc[r, h * 128 : h * 128 + 128])
-            k_unit, k_inv = unit(acc[r, 256 + h * 128 : 384 + h * 128])
-            value = acc[r, 512 + h * 128 : 640 + h * 128].astype(BF16)
+            q_unit, q_inv = unit(projected(image, h * 128))
+            k_unit, k_inv = unit(projected(image, 256 + h * 128))
+            value = projected(image, 512 + h * 128).astype(BF16)
             qn, kn = (q_unit * q_gain).astype(BF16), (k_unit * k_gain).astype(BF16)
             cot = go[r, h * 128 : h * 128 + 128]
             scores = dot(qn, kn, ((1,), (1,))) * (128**-0.5)
@@ -384,7 +412,7 @@
             pltpu.VMEM((8, 768, 384), BF16),
             pltpu.VMEM((6, 768, 384), BF16),
             pltpu.VMEM((768, 384), BF16),
-            pltpu.VMEM((512, 768), F32),
+            pltpu.VMEM((8, 64, 768), F32),
             pltpu.VMEM((512, 768), BF16),
             pltpu.VMEM((768, 512), BF16),
             pltpu.VMEM((512, 256), BF16),

time: 129 us -> 125 us (0.969)
  Pallas kernels: 127 us -> 124 us
    pallas_call x1, Pallas kernels: 125 us -> 122 us  [per_device(): pl.pallas_call(kernel, out_shape=shapes, in_specs=[anywhere] + [vmem] * 3...]
where the time goes in v4:
time: 125 us
  Pallas kernels  124 us (99%)
    pallas_call x1, Pallas kernels, per_device(): pl.pallas_call(kernel, out_shape=shapes, in_specs=[anywhere] + [vmem] * 3...  122 us

profile of v4, /device:TPU:32, one launch (start us, length us, event | category | flops | bytes accessed | tf_op | source)
XLA Modules:
  0.0 125.2 jit_solution(1165562345369130372)
XLA Ops:
  0.6 122.3 %attention_branch_back.1 = (bf16[32,6144]{1,0:T(8,128)(2,1)}, bf16[384,256]{1,0:T(8,128)(2,1)}, bf16[384,256]{1,0:T(8,128)(2,1)}, bf16[384,256]{1,0:T(8,128)(2,1)}) custom-call(bf16[32,6144]{1,0:T(8,128)(2,1)} %tok_in.1, f32[1,6144]{1,0:T(1,128)} %bitcast.3, f32[1,128]{1,0:T(1,128)} %bitcast.4, f32[1,128]{1,0:T(1,128)} %bitcast.5, bf16[384,256]{1,0:T(8,128)(2,1)} %wq.1, ...), custom_call_target="tpu_custom_call" | custom-call | flops 15000000512 | bytes 3000000 | tf_op jit(solution)/shard_map/attention_branch_back/pallas_call | solution.py:397
  122.9 2.2 %hand_on.1 = (bf16[32,6144]{1,0:T(8,128)(2,1)}, bf16[384,256]{1,0:T(8,128)(2,1)}, bf16[384,256]{1,0:T(8,128)(2,1)}, bf16[384,256]{1,0:T(8,128)(2,1)}) custom-call(bf16[32,6144]{1,0:T(8,128)(2,1)} %get-tuple-element.8.refs_0_, bf16[384,256]{1,0:T(8,128)(2,1)} %get-tuple-element.9.refs_1_, bf16[384,256]{1,0:T(8,128)(2,1)} %get-tuple-element.10.refs_2_, ...), custom_call_target="tpu_custom_call" | custom-call | tf_op jit(solution)/shard_map/hand_on/pallas_call | solution.py:433

commit v5 on v4

--- a/solution.py
+++ b/solution.py
@@ -207,6 +207,8 @@
         elif event == "near2":
             sibling_weights(("f1", "b1"), 1)
             project_near(((1, 1), (1, -1)))
+            sibling_weights(("f2",), 1)
+            project_near(((1, 2),))
         elif event[0] == "o":
             got(f"x{event}", nrm.at[z, 1 - xl, :, span(event[1:])])
             put_z(event[1:])
@@ -221,10 +223,8 @@
         else:
             tokens_step(event[:2], event[2], int(event[3]))
     over_x(3, 4)
-    got("wsf21", wts.at[dp(1, yo(2), 1 - core)])
     far = jnp.concatenate([nrm[zo(q)].reshape(64, 6144) for q in (3, 4, -3)], axis=0)
     acc[3:6] = dot(far, wts[...].reshape(6144, 768), ((1,), (0,))).reshape(3, 64, 768)
-    project_near(((1, 2),))
 
     heads_in.wait()
     q_gain, k_gain = qg[...], kg[...]

time: 125 us -> 125 us (level)
  no operation moved by 1% of the time
where the time goes in v5:
time: 125 us
  Pallas kernels  124 us (99%)
    pallas_call x1, Pallas kernels, per_device(): pl.pallas_call(kernel, out_shape=shapes, in_specs=[anywhere] + [vmem] * 3...  122 us

profile of v5, /device:TPU:32, one launch (start us, length us, event | category | flops | bytes accessed | tf_op | source)
XLA Modules:
  0.0 124.7 jit_solution(10141916189800300676)
XLA Ops:
  0.6 121.7 %attention_branch_back.1 = (bf16[32,6144]{1,0:T(8,128)(2,1)}, bf16[384,256]{1,0:T(8,128)(2,1)}, bf16[384,256]{1,0:T(8,128)(2,1)}, bf16[384,256]{1,0:T(8,128)(2,1)}) custom-call(bf16[32,6144]{1,0:T(8,128)(2,1)} %tok_in.1, f32[1,6144]{1,0:T(1,128)} %bitcast.3, f32[1,128]{1,0:T(1,128)} %bitcast.4, f32[1,128]{1,0:T(1,128)} %bitcast.5, bf16[384,256]{1,0:T(8,128)(2,1)} %wq.1, ...), custom_call_target="tpu_custom_call" | custom-call | flops 15000000512 | bytes 3000000 | tf_op jit(solution)/shard_map/attention_branch_back/pallas_call | solution.py:397
  122.4 2.2 %hand_on.1 = (bf16[32,6144]{1,0:T(8,128)(2,1)}, bf16[384,256]{1,0:T(8,128)(2,1)}, bf16[384,256]{1,0:T(8,128)(2,1)}, bf16[384,256]{1,0:T(8,128)(2,1)}) custom-call(bf16[32,6144]{1,0:T(8,128)(2,1)} %get-tuple-element.8.refs_0_, bf16[384,256]{1,0:T(8,128)(2,1)} %get-tuple-element.9.refs_1_, bf16[384,256]{1,0:T(8,128)(2,1)} %get-tuple-element.10.refs_2_, ...), custom_call_target="tpu_custom_call" | custom-call | tf_op jit(solution)/shard_map/hand_on/pallas_call | solution.py:433
